TPU v7x, 512 devices: a whole 4x4x16 slice. The times are simulated.
512 devices in a mesh: gx: 32 (over z, core), gy: 16 (over y, x).
Axes of the slice: x: 4, y: 4, z: 16, core: 2. Of those that a mesh axis runs over, the one named last changes fastest.
Arguments:
- residual: float32 [3, 512, 256, 128], P(None, 'gx', 'gy'), may hold values from -6 to 6
- stiffness: float32 [512, 256], P('gx', 'gy'), may hold values from 0.5 to 2
- local_inverse: bfloat16 [32, 16, 1024, 1024], P('gx', 'gy'), as said below
- coarse_basis: bfloat16 [32, 16, 8, 1024], P('gx', 'gy'), may hold values from -0.5 to 0.5
- coarse_rows: bfloat16 [32, 16, 8, 4096], P('gx', 'gy'), as said below
- send_rows: int32 [32, 16, 4, 64], P('gx', 'gy'), may hold values from 0 to 767, as said below
- partition_map: int32 [512], replicated, may hold values from 0 to 511, as said below
Outputs:
- solution: float32 [3, 512, 256, 128], P(None, 'gx', 'gy')
- final: float32 [3, 512, 256, 128], P(None, 'gx', 'gy')
Inputs may be any that keep to these rules, and one draw needn't show every extreme that they name: `send_rows`: for each subdomain, the lists j = 0, 1 (lower and upper neighbour along gx) and j = 2, 3 (lower and upper neighbour along gy) each name 64 distinct owned rows, all of them in the two layers of cells nearest that neighbour. `partition_map`: A permutation of the device numbers. `coarse_rows`: with its columns put in device order through partition_map, the 4096-square matrix S is symmetric. `local_inverse`: each subdomain's block is symmetric.
All inputs are finite; a program needn't handle non-finite values.
Results may differ from a plain program's by a relative error of at most 0.0057.
Values may be sent and summed in bfloat16 or wider, within the bound.
No kernel may reach another device: no remote copies, remote signals or barrier semaphores. Data moves between devices by JAX's collectives and lax.ppermute only.
A program may use at most 64 MiB of HBM per device.

v0:
```python
import jax
import jax.numpy as jnp
from jax import lax
from jax.sharding import PartitionSpec as P


def with_halo(block, sides, width):
    for axis, dim in sides:
        count = lax.axis_size(axis)
        forward = [(i, i + 1) for i in range(count - 1)]
        backward = [(target, source) for source, target in forward]
        low = lax.ppermute(
            lax.slice_in_dim(block, block.shape[dim] - width, None, axis=dim), axis, forward
        )
        high = lax.ppermute(lax.slice_in_dim(block, 0, width, axis=dim), axis, backward)
        block = jnp.concatenate([low, block, high], axis=dim)
    return block


def trade_along_gx(pair):
    return with_halo(pair, (("gx", 0),), 1)


def trade_along_gy(pair):
    return with_halo(pair, (("gy", 0),), 1)


def operate(values, stiffness):
    padded = with_halo(values, (("gx", 1), ("gy", 2)), 1)
    beside = padded[:, 2:, 1:-1] + padded[:, :-2, 1:-1] + padded[:, 1:-1, 2:] + padded[:, 1:-1, :-2]
    return (4.0 + stiffness[None, :, :, None]) * values - beside


def coarse_solve(coarse_in, ordered):
    return jnp.dot(
        ordered,
        lax.all_gather(coarse_in, ("gx", "gy"), axis=0, tiled=True),
        preferred_element_type=jnp.float32,
    )


def precondition(values, inverse, basis_rows, row_lists, ordered):
    own_rows = values.reshape(-1, values.shape[-1])
    own_count = own_rows.shape[0]
    margin = row_lists.shape[1]
    outgoing = jnp.take(own_rows, row_lists, axis=0)
    from_gx = trade_along_gx(outgoing[0:2])
    from_gy = trade_along_gy(outgoing[2:4])
    subdomain = jnp.concatenate([own_rows, from_gx[0], from_gx[3], from_gy[0], from_gy[3]], axis=0)
    subdomain = subdomain.astype(jnp.bfloat16)
    coarse_in = jnp.dot(basis_rows, subdomain, preferred_element_type=jnp.float32).astype(
        jnp.bfloat16
    )
    coarse_out = coarse_solve(coarse_in, ordered).astype(jnp.bfloat16)
    patch = jnp.dot(inverse, subdomain, preferred_element_type=jnp.float32)
    patch = patch + lax.dot_general(
        basis_rows, coarse_out, (((0,), (0,)), ((), ())), preferred_element_type=jnp.float32
    )
    back_gx = trade_along_gx(
        jnp.stack(
            [
                patch[own_count : own_count + margin],
                patch[own_count + margin : own_count + 2 * margin],
            ]
        )
    )
    back_gy = trade_along_gy(
        jnp.stack(
            [
                patch[own_count + 2 * margin : own_count + 3 * margin],
                patch[own_count + 3 * margin :],
            ]
        )
    )
    update = patch[:own_count]
    update = update.at[row_lists[0]].add(back_gx[0])
    update = update.at[row_lists[1]].add(back_gx[3])
    update = update.at[row_lists[2]].add(back_gy[0])
    update = update.at[row_lists[3]].add(back_gy[3])
    return update.reshape(values.shape)


def per_device(
    residual, stiffness, local_inverse, coarse_basis, coarse_rows, send_rows, partition_map
):
    inverse = local_inverse[0, 0]
    basis_rows = coarse_basis[0, 0]
    row_lists = send_rows[0, 0]
    device_count = partition_map.shape[0]
    coarse_width = basis_rows.shape[0]
    stored = coarse_rows[0, 0].reshape(coarse_width, device_count, coarse_width)
    ordered = jnp.take(stored, partition_map, axis=1).reshape(
        coarse_width, device_count * coarse_width
    )
    first_pass = precondition(residual, inverse, basis_rows, row_lists, ordered)
    middle = residual - operate(first_pass, stiffness)
    second_pass = precondition(middle, inverse, basis_rows, row_lists, ordered)
    solution = first_pass + second_pass
    return (solution, residual - operate(solution, stiffness))


def solution(mesh):
    placed = (
        P(None, "gx", "gy", None),
        P("gx", "gy"),
        P("gx", "gy", None, None),
        P("gx", "gy", None, None),
        P("gx", "gy", None, None),
        P("gx", "gy", None, None),
        P(),
    )
    return jax.shard_map(
        per_device,
        mesh=mesh,
        in_specs=placed,
        out_specs=(P(None, "gx", "gy", None), P(None, "gx", "gy", None)),
        check_vma=False,
    )
```

profile of v0, /device:TPU:40, one launch (start us, length us, event | category | flops | bytes accessed | tf_op | source)
XLA Modules:
  0.0 486.4 jit_solution(15836216177516421753)
XLA Ops:
  11.4 1.9 collective-permute-start
  13.3 3.6 collective-permute-start.1
  16.9 3.4 collective-permute-start.2
  20.4 4.6 collective-permute-start.3
  27.9 3.0 reshape_squeeze.3
  32.8 2.4 gather_fusion
  38.4 163.3 %all-gather.3.cloned.1.call-done = bf16[4096,128]{1,0:T(8,128)(2,1)} async-done(((bf16[8,128]{1,0:T(8,128)(2,1)}), bf16[4096,128]{1,0:T(8,128)(2,1)}) %all-gather.3.cloned.1.call-update) | async-done | bytes 1048592 | tf_op jit(solution)/shard_map/all_gather | solution.py:37
  205.0 2.1 collective-permute-start.4
  207.2 3.4 collective-permute-start.5
  210.6 3.3 collective-permute-start.6
  213.9 4.7 collective-permute-start.7
  225.7 1.9 collective-permute-start.8
  227.6 2.4 collective-permute-start.9
  230.1 2.7 collective-permute-done.9
  232.8 6.3 %collective-permute-start.10 = (f32[3,18,1,128]{3,2,1,0:T(1,128)S(1)}, f32[3,18,1,128]{3,2,1,0:T(1,128)S(1)}, u32[]{:S(2)}, u32[]{:S(2)}) collective-permute-start(f32[3,18,1,128]{3,2,1,0:T(1,128)S(1)} %get-tuple-element.13), channel_id=1, source_target_pairs={{1,0},{2,1},{3,2},{4,3},{5,4},{6,5},{7,6},{8,7},{9,8},{10,9},{11,1... | collective-permute-start | bytes 82952 | tf_op jit(solution)/shard_map/ppermute | solution.py:15
  239.1 1.9 collective-permute-start.11
  241.1 5.9 %collective-permute-done.11 = f32[3,18,1,128]{3,2,1,0:T(1,128)S(1)} collective-permute-done((f32[3,18,1,128]{3,2,1,0:T(1,128)S(1)}, f32[3,18,1,128]{3,2,1,0:T(1,128)S(1)}, u32[]{:S(2)}, u32[]{:S(2)}) %collective-permute-start.11) | collective-permute-done | bytes 27680 | tf_op jit(solution)/shard_map/ppermute | solution.py:12
  248.2 1.9 collective-permute-start.12
  250.1 3.6 collective-permute-start.13
  253.8 1.9 collective-permute-start.14
  255.7 6.0 %collective-permute-start.15 = (bf16[1,64,128]{2,1,0:T(8,128)(2,1)S(1)}, bf16[1,64,128]{2,1,0:T(8,128)(2,1)S(1)}, u32[]{:S(2)}, u32[]{:S(2)}) collective-permute-start(bf16[1,64,128]{2,1,0:T(8,128)(2,1)S(1)} %get-tuple-element.19), channel_id=1, source_target_pairs={{1,0},{2,1},{3,2},{4,3},{5,4},{6,5},{7,6},{8,7},{9,8},{10,9},{11,1... | collective-permute-start | bytes 49160 | tf_op jit(solution)/shard_map/ppermute | solution.py:15
  264.6 168.2 %all-gather.5.cloned.1.call-done = bf16[4096,128]{1,0:T(8,128)(2,1)} async-done(((bf16[8,128]{1,0:T(8,128)(2,1)}), bf16[4096,128]{1,0:T(8,128)(2,1)}) %all-gather.5.cloned.1.call-update) | async-done | bytes 1048592 | tf_op jit(solution)/shard_map/all_gather | solution.py:37
  437.1 2.1 collective-permute-start.16
  439.3 3.4 collective-permute-start.17
  442.7 3.3 collective-permute-start.18
  446.0 4.7 collective-permute-start.19
  461.2 1.9 collective-permute-start.20
  463.1 2.4 collective-permute-start.21
  465.5 2.7 collective-permute-done.21
  468.3 2.5 collective-permute-start.22
  470.8 3.4 collective-permute-start.23
  474.2 4.5 collective-permute-done.23
  (128 shorter events, 42.2 us)
Async XLA Ops:
  7.2 196.3 %copy-start = (bf16[1,1,1024,1024]{3,2,1,0:T(8,128)(2,1)S(1)}, bf16[1,1,1024,1024]{3,2,1,0:T(8,128)(2,1)}, u32[]{:S(2)}) copy-start(bf16[1,1,1024,1024]{3,2,1,0:T(8,128)(2,1)} %param.11) | copy-start | bytes 6291460
  7.2 194.5 %all-gather.3.cloned.1.call-start = ((), (), s32[]{:S(2)}) async-start(), calls=%async_computation | async-start | bytes 1050624 | tf_op jit(solution)/shard_map/all_gather | solution.py:37
  11.4 14.6 %collective-permute-start = (bf16[1,64,128]{2,1,0:T(8,128)(2,1)S(1)}, bf16[1,64,128]{2,1,0:T(8,128)(2,1)S(1)}, u32[]{:S(2)}, u32[]{:S(2)}) collective-permute-start(bf16[1,64,128]{2,1,0:T(8,128)(2,1)S(1)} %get-tuple-element.26), channel_id=1, source_target_pairs={{0,16},{16,32},{32,48},{48,64},{64,80},{80,96},{96,112},{112,128},... | collective-permute-start | bytes 49160 | tf_op jit(solution)/shard_map/ppermute | solution.py:12
  13.3 12.7 %collective-permute-start.1 = (bf16[1,64,128]{2,1,0:T(8,128)(2,1)S(1)}, bf16[1,64,128]{2,1,0:T(8,128)(2,1)S(1)}, u32[]{:S(2)}, u32[]{:S(2)}) collective-permute-start(bf16[1,64,128]{2,1,0:T(8,128)(2,1)S(1)} %get-tuple-element.25), channel_id=1, source_target_pairs={{16,0},{32,16},{48,32},{64,48},{80,64},{96,80},{112,96},{128,112},... | collective-permute-start | bytes 49160 | tf_op jit(solution)/shard_map/ppermute | solution.py:15
  16.9 9.1 %collective-permute-start.2 = (bf16[1,64,128]{2,1,0:T(8,128)(2,1)S(1)}, bf16[1,64,128]{2,1,0:T(8,128)(2,1)S(1)}, u32[]{:S(2)}, u32[]{:S(2)}) collective-permute-start(bf16[1,64,128]{2,1,0:T(8,128)(2,1)S(1)} %get-tuple-element.24), channel_id=1, source_target_pairs={{0,1},{1,2},{2,3},{3,4},{4,5},{5,6},{6,7},{7,8},{8,9},{9,10},{10,1... | collective-permute-start | bytes 49160 | tf_op jit(solution)/shard_map/ppermute | solution.py:12
  20.4 6.0 %collective-permute-start.3 = (bf16[1,64,128]{2,1,0:T(8,128)(2,1)S(1)}, bf16[1,64,128]{2,1,0:T(8,128)(2,1)S(1)}, u32[]{:S(2)}, u32[]{:S(2)}) collective-permute-start(bf16[1,64,128]{2,1,0:T(8,128)(2,1)S(1)} %get-tuple-element.23), channel_id=1, source_target_pairs={{1,0},{2,1},{3,2},{4,3},{5,4},{6,5},{7,6},{8,7},{9,8},{10,9},{11,1... | collective-permute-start | bytes 49160 | tf_op jit(solution)/shard_map/ppermute | solution.py:15
  27.8 405.0 %all-gather.5.cloned.1.call-start = ((), (), s32[]{:S(2)}) async-start(), calls=%async_computation.1 | async-start | bytes 1050624 | tf_op jit(solution)/shard_map/all_gather | solution.py:37
  35.2 166.5 %copy-start.4 = (bf16[1,1,8,1024]{3,2,1,0:T(8,128)(2,1)S(1)}, bf16[1,1,8,1024]{3,2,1,0:T(8,128)(2,1)}, u32[]{:S(2)}) copy-start(bf16[1,1,8,1024]{3,2,1,0:T(8,128)(2,1)} %param.12) | copy-start | bytes 49156
  38.4 165.9 %copy-start.7 = (pred[4096]{0:T(1024)(128)(4,1)}, pred[4096]{0:T(1024)(128)(4,1)S(1)}, u32[]{:S(2)}) copy-start(pred[4096]{0:T(1024)(128)(4,1)S(1)} %broadcast_in_dim.36) | copy-start | bytes 12292
  205.0 14.4 %collective-permute-start.4 = (f32[1,64,128]{1,2,0:T(8,128)}, f32[1,64,128]{1,2,0:T(8,128)}, u32[]{:S(2)}, u32[]{:S(2)}) collective-permute-start(f32[1,64,128]{1,2,0:T(8,128)} %get-tuple-element.10), channel_id=1, source_target_pairs={{0,16},{16,32},{32,48},{48,64},{64,80},{80,96},{96,112},{112,128},... | collective-permute-start | bytes 98312 | tf_op jit(solution)/shard_map/ppermute | solution.py:12
  207.2 13.1 %collective-permute-start.5 = (f32[1,64,128]{1,2,0:T(8,128)}, f32[1,64,128]{1,2,0:T(8,128)S(1)}, u32[]{:S(2)}, u32[]{:S(2)}) collective-permute-start(f32[1,64,128]{1,2,0:T(8,128)} %get-tuple-element.9), channel_id=1, source_target_pairs={{16,0},{32,16},{48,32},{64,48},{80,64},{96,80},{112,96},{128,112},... | collective-permute-start | bytes 98312 | tf_op jit(solution)/shard_map/ppermute | solution.py:15
  210.6 9.8 %collective-permute-start.6 = (f32[1,64,128]{1,2,0:T(8,128)}, f32[1,64,128]{1,2,0:T(8,128)S(1)}, u32[]{:S(2)}, u32[]{:S(2)}) collective-permute-start(f32[1,64,128]{1,2,0:T(8,128)} %get-tuple-element.8), channel_id=1, source_target_pairs={{0,1},{1,2},{2,3},{3,4},{4,5},{5,6},{6,7},{7,8},{8,9},{9,10},{10,1... | collective-permute-start | bytes 98312 | tf_op jit(solution)/shard_map/ppermute | solution.py:12
  213.9 6.9 %collective-permute-start.7 = (f32[1,64,128]{1,2,0:T(8,128)}, f32[1,64,128]{1,2,0:T(8,128)S(1)}, u32[]{:S(2)}, u32[]{:S(2)}) collective-permute-start(f32[1,64,128]{1,2,0:T(8,128)} %get-tuple-element.7), channel_id=1, source_target_pairs={{1,0},{2,1},{3,2},{4,3},{5,4},{6,5},{7,6},{8,7},{9,8},{10,9},{11,1... | collective-permute-start | bytes 98312 | tf_op jit(solution)/shard_map/ppermute | solution.py:15
  219.2 27.8 %copy-start.1 = (f32[3,16,16,128]{3,2,1,0:T(8,128)S(1)}, f32[3,16,16,128]{3,2,1,0:T(8,128)}, u32[]{:S(2)}) copy-start(f32[3,16,16,128]{3,2,1,0:T(8,128)} %param.9) | copy-start | bytes 1179652
  220.4 26.8 %copy-start.11 = (s32[1024]{0:T(1024)S(1)}, s32[1024]{0:T(1024)}, u32[]{:S(2)}) copy-start(s32[1024]{0:T(1024)} %copy-done.10) | copy-start | bytes 12292
  224.5 208.3 %copy-start.8 = (pred[4096]{0:T(1024)(128)(4,1)S(1)}, pred[4096]{0:T(1024)(128)(4,1)}, u32[]{:S(2)}) copy-start(pred[4096]{0:T(1024)(128)(4,1)} %copy-done.7) | copy-start | bytes 12292
  225.7 4.3 collective-permute-start.8
  227.6 5.1 %collective-permute-start.9 = (f32[3,1,16,128]{3,2,1,0:T(8,128)S(1)}, f32[3,1,16,128]{3,2,1,0:T(8,128)S(1)}, u32[]{:S(2)}, u32[]{:S(2)}) collective-permute-start(f32[3,1,16,128]{3,2,1,0:T(8,128)S(1)} %get-tuple-element.17), channel_id=1, source_target_pairs={{0,16},{16,32},{32,48},{48,64},{64,80},{80,96},{96,112},{112,128},... | collective-permute-start | bytes 73736 | tf_op jit(solution)/shard_map/ppermute | solution.py:12
  232.8 8.2 %collective-permute-start.10 = (f32[3,18,1,128]{3,2,1,0:T(1,128)S(1)}, f32[3,18,1,128]{3,2,1,0:T(1,128)S(1)}, u32[]{:S(2)}, u32[]{:S(2)}) collective-permute-start(f32[3,18,1,128]{3,2,1,0:T(1,128)S(1)} %get-tuple-element.13), channel_id=1, source_target_pairs={{1,0},{2,1},{3,2},{4,3},{5,4},{6,5},{7,6},{8,7},{9,8},{10,9},{11,1... | collective-permute-start | bytes 82952 | tf_op jit(solution)/shard_map/ppermute | solution.py:15
  239.1 7.9 %collective-permute-start.11 = (f32[3,18,1,128]{3,2,1,0:T(1,128)S(1)}, f32[3,18,1,128]{3,2,1,0:T(1,128)S(1)}, u32[]{:S(2)}, u32[]{:S(2)}) collective-permute-start(f32[3,18,1,128]{3,2,1,0:T(1,128)S(1)} %get-tuple-element.14), channel_id=1, source_target_pairs={{0,1},{1,2},{2,3},{3,4},{4,5},{5,6},{6,7},{7,8},{8,9},{9,10},{10,1... | collective-permute-start | bytes 82952 | tf_op jit(solution)/shard_map/ppermute | solution.py:12
  248.2 13.6 %collective-permute-start.12 = (bf16[1,64,128]{2,1,0:T(8,128)(2,1)S(1)}, bf16[1,64,128]{2,1,0:T(8,128)(2,1)S(1)}, u32[]{:S(2)}, u32[]{:S(2)}) collective-permute-start(bf16[1,64,128]{2,1,0:T(8,128)(2,1)S(1)} %get-tuple-element.22), channel_id=1, source_target_pairs={{0,16},{16,32},{32,48},{48,64},{64,80},{80,96},{96,112},{112,128},... | collective-permute-start | bytes 49160 | tf_op jit(solution)/shard_map/ppermute | solution.py:12
  250.1 11.6 %collective-permute-start.13 = (bf16[1,64,128]{2,1,0:T(8,128)(2,1)S(1)}, bf16[1,64,128]{2,1,0:T(8,128)(2,1)S(1)}, u32[]{:S(2)}, u32[]{:S(2)}) collective-permute-start(bf16[1,64,128]{2,1,0:T(8,128)(2,1)S(1)} %get-tuple-element.21), channel_id=1, source_target_pairs={{16,0},{32,16},{48,32},{64,48},{80,64},{96,80},{112,96},{128,112},... | collective-permute-start | bytes 49160 | tf_op jit(solution)/shard_map/ppermute | solution.py:15
  253.8 8.0 %collective-permute-start.14 = (bf16[1,64,128]{2,1,0:T(8,128)(2,1)S(1)}, bf16[1,64,128]{2,1,0:T(8,128)(2,1)S(1)}, u32[]{:S(2)}, u32[]{:S(2)}) collective-permute-start(bf16[1,64,128]{2,1,0:T(8,128)(2,1)S(1)} %get-tuple-element.20), channel_id=1, source_target_pairs={{0,1},{1,2},{2,3},{3,4},{4,5},{5,6},{6,7},{7,8},{8,9},{9,10},{10,1... | collective-permute-start | bytes 49160 | tf_op jit(solution)/shard_map/ppermute | solution.py:12
  255.7 7.5 %collective-permute-start.15 = (bf16[1,64,128]{2,1,0:T(8,128)(2,1)S(1)}, bf16[1,64,128]{2,1,0:T(8,128)(2,1)S(1)}, u32[]{:S(2)}, u32[]{:S(2)}) collective-permute-start(bf16[1,64,128]{2,1,0:T(8,128)(2,1)S(1)} %get-tuple-element.19), channel_id=1, source_target_pairs={{1,0},{2,1},{3,2},{4,3},{5,4},{6,5},{7,6},{8,7},{9,8},{10,9},{11,1... | collective-permute-start | bytes 49160 | tf_op jit(solution)/shard_map/ppermute | solution.py:15
  437.1 15.5 %collective-permute-start.16 = (f32[1,64,128]{1,2,0:T(8,128)}, f32[1,64,128]{1,2,0:T(8,128)S(1)}, u32[]{:S(2)}, u32[]{:S(2)}) collective-permute-start(f32[1,64,128]{1,2,0:T(8,128)} %get-tuple-element.6), channel_id=1, source_target_pairs={{0,16},{16,32},{32,48},{48,64},{64,80},{80,96},{96,112},{112,128},... | collective-permute-start | bytes 98312 | tf_op jit(solution)/shard_map/ppermute | solution.py:12
  439.3 14.9 %collective-permute-start.17 = (f32[1,64,128]{1,2,0:T(8,128)}, f32[1,64,128]{1,2,0:T(8,128)}, u32[]{:S(2)}, u32[]{:S(2)}) collective-permute-start(f32[1,64,128]{1,2,0:T(8,128)} %get-tuple-element.5), channel_id=1, source_target_pairs={{16,0},{32,16},{48,32},{64,48},{80,64},{96,80},{112,96},{128,112},... | collective-permute-start | bytes 98312 | tf_op jit(solution)/shard_map/ppermute | solution.py:15
  442.7 12.4 %collective-permute-start.18 = (f32[1,64,128]{1,2,0:T(8,128)}, f32[1,64,128]{1,2,0:T(8,128)S(1)}, u32[]{:S(2)}, u32[]{:S(2)}) collective-permute-start(f32[1,64,128]{1,2,0:T(8,128)} %get-tuple-element.4), channel_id=1, source_target_pairs={{0,1},{1,2},{2,3},{3,4},{4,5},{5,6},{6,7},{7,8},{8,9},{9,10},{10,1... | collective-permute-start | bytes 98312 | tf_op jit(solution)/shard_map/ppermute | solution.py:12
  446.0 10.7 %collective-permute-start.19 = (f32[1,64,128]{1,2,0:T(8,128)}, f32[1,64,128]{1,2,0:T(8,128)S(1)}, u32[]{:S(2)}, u32[]{:S(2)}) collective-permute-start(f32[1,64,128]{1,2,0:T(8,128)} %get-tuple-element.3), channel_id=1, source_target_pairs={{1,0},{2,1},{3,2},{4,3},{5,4},{6,5},{7,6},{8,7},{9,8},{10,9},{11,1... | collective-permute-start | bytes 98312 | tf_op jit(solution)/shard_map/ppermute | solution.py:15
  461.2 4.3 collective-permute-start.20
  463.1 5.1 %collective-permute-start.21 = (f32[3,1,16,128]{3,2,1,0:T(8,128)S(1)}, f32[3,1,16,128]{3,2,1,0:T(8,128)S(1)}, u32[]{:S(2)}, u32[]{:S(2)}) collective-permute-start(f32[3,1,16,128]{3,2,1,0:T(8,128)S(1)} %get-tuple-element.15), channel_id=1, source_target_pairs={{0,16},{16,32},{32,48},{48,64},{64,80},{80,96},{96,112},{112,128},... | collective-permute-start | bytes 73736 | tf_op jit(solution)/shard_map/ppermute | solution.py:12
  468.3 5.9 %collective-permute-start.22 = (f32[3,18,1,128]{3,2,1,0:T(1,128)S(1)}, f32[3,18,1,128]{3,2,1,0:T(1,128)S(1)}, u32[]{:S(2)}, u32[]{:S(2)}) collective-permute-start(f32[3,18,1,128]{3,2,1,0:T(1,128)S(1)} %get-tuple-element.11), channel_id=1, source_target_pairs={{1,0},{2,1},{3,2},{4,3},{5,4},{6,5},{7,6},{8,7},{9,8},{10,9},{11,1... | collective-permute-start | bytes 82952 | tf_op jit(solution)/shard_map/ppermute | solution.py:15
  470.8 7.9 %collective-permute-start.23 = (f32[3,18,1,128]{3,2,1,0:T(1,128)S(1)}, f32[3,18,1,128]{3,2,1,0:T(1,128)S(1)}, u32[]{:S(2)}, u32[]{:S(2)}) collective-permute-start(f32[3,18,1,128]{3,2,1,0:T(1,128)S(1)} %get-tuple-element.12), channel_id=1, source_target_pairs={{0,1},{1,2},{2,3},{3,4},{4,5},{5,6},{6,7},{7,8},{8,9},{9,10},{10,1... | collective-permute-start | bytes 82952 | tf_op jit(solution)/shard_map/ppermute | solution.py:12
  (14 other events, 196.6 us)
Sparse Core Ops, SparseCore 0:
  28.0 173.6 all-gather.2
  264.8 168.0 all-gather.4
where the time goes:
time: 488 us; the launch traced here: 486 us
  waiting for transfers between devices  349 us (72%)
  starting transfers between devices  76.8 us (16%)
  local copies, waits for them, and re-layouts  22.8 us (5%)
  between operations  14.8 us (3%)
  other arithmetic  14.4 us (3%)
  matrix products  8.25 us (2%)
    all_gather x2, waiting for transfers between devices, coarse_solve(): lax.all_gather(coarse_in, ('gx', 'gy'), axis=0, tiled=True)  331 us
    ppermute x12, starting transfers between devices, with_halo(): lax.ppermute(lax.slice_in_dim(block, 0, width, axis=dim), axis, backward)  46.6 us
    ppermute x12, starting transfers between devices, with_halo(): lax.ppermute(lax.slice_in_dim(block, block.shape[dim] - width, None, axis...  30.1 us
    ppermute x12, waiting for transfers between devices, with_halo(): lax.ppermute(lax.slice_in_dim(block, block.shape[dim] - width, None, axis...  15.9 us
  transfers between devices with their start and end apart: 26, of which 9 were waited for; matrix products, arithmetic and copies ran while one was open for 4% of the time, Pallas kernels for 0%

commit v1 on v0

--- a/solution.py
+++ b/solution.py
@@ -2,6 +2,16 @@
 import jax.numpy as jnp
 from jax import lax
 from jax.sharding import PartitionSpec as P
+
+number_the_joints = lambda w_in: jnp.concatenate(
+    jax.lax.all_to_all(
+        jnp.stack(jax.lax.axis_size(("gx", "gy")) * [w_in]),
+        axis_name=("gx", "gy"),
+        split_axis=0,
+        concat_axis=0,
+    ),
+    axis=0,
+)
 
 
 def with_halo(block, sides, width):
@@ -32,11 +42,7 @@
 
 
 def coarse_solve(coarse_in, ordered):
-    return jnp.dot(
-        ordered,
-        lax.all_gather(coarse_in, ("gx", "gy"), axis=0, tiled=True),
-        preferred_element_type=jnp.float32,
-    )
+    return jnp.dot(ordered, number_the_joints(coarse_in), preferred_element_type=jnp.float32)
 
 
 def precondition(values, inverse, basis_rows, row_lists, ordered):

time: 488 us -> 283 us (0.58)
  the two profiles are of different devices: /device:TPU:40 before, /device:TPU:9 now
where the time goes in v1:
time: 283 us; the launch traced here: 281 us
  starting transfers between devices  100 us (35%)
  blocking collectives  69 us (24%)
  waiting for transfers between devices  67.7 us (24%)
  local copies, waits for them, and re-layouts  16.4 us (6%)
  other arithmetic  13.8 us (5%)
  matrix products  12.6 us (4%)
    all_to_all x1, blocking collectives, jax.lax.all_to_all(jnp.stack(jax.lax.axis_size(('gx', 'gy')) * [w_in]), a...  69 us
    all_to_all x1, waiting for transfers between devices, jax.lax.all_to_all(jnp.stack(jax.lax.axis_size(('gx', 'gy')) * [w_in]), a...  48 us
    ppermute x12, starting transfers between devices, with_halo(): lax.ppermute(lax.slice_in_dim(block, 0, width, axis=dim), axis, backward)  40.3 us
    ppermute x12, starting transfers between devices, with_halo(): lax.ppermute(lax.slice_in_dim(block, block.shape[dim] - width, None, axis...  32.2 us
    all_to_all x1, starting transfers between devices, jax.lax.all_to_all(jnp.stack(jax.lax.axis_size(('gx', 'gy')) * [w_in]), a...  28 us
    ppermute x12, waiting for transfers between devices, with_halo(): lax.ppermute(lax.slice_in_dim(block, block.shape[dim] - width, None, axis...  10.1 us
    ppermute x12, waiting for transfers between devices, with_halo(): lax.ppermute(lax.slice_in_dim(block, 0, width, axis=dim), axis, backward)  9.57 us
    dot_general x2, matrix products, precondition(): lax.dot_general(basis_rows, coarse_out, (((0,), (0,)), ((), ())), preferr...  8.62 us
  transfers between devices with their start and end apart: 25, of which 7 were waited for; matrix products, arithmetic and copies ran while one was open for 4% of the time, Pallas kernels for 0%

profile of v1, /device:TPU:9, one launch (start us, length us, event | category | flops | bytes accessed | tf_op | source)
XLA Modules:
  0.0 281.4 jit_solution(17233942499902118376)
XLA Ops:
  4.1 4.3 %collective-permute-start.3 = (bf16[1,64,128]{2,1,0:T(8,128)(2,1)S(1)}, bf16[1,64,128]{2,1,0:T(8,128)(2,1)S(1)}, u32[]{:S(2)}, u32[]{:S(2)}) collective-permute-start(bf16[1,64,128]{2,1,0:T(8,128)(2,1)S(1)} %get-tuple-element.23), channel_id=1, source_target_pairs={{1,0},{2,1},{3,2},{4,3},{5,4},{6,5},{7,6},{8,7},{9,8},{10,9},{11,1... | collective-permute-start | bytes 49160 | tf_op jit(solution)/shard_map/ppermute | solution.py:25
  8.4 1.9 collective-permute-start.2
  10.3 2.9 %collective-permute-start.1 = (bf16[1,64,128]{2,1,0:T(8,128)(2,1)S(1)}, bf16[1,64,128]{2,1,0:T(8,128)(2,1)S(1)}, u32[]{:S(2)}, u32[]{:S(2)}) collective-permute-start(bf16[1,64,128]{2,1,0:T(8,128)(2,1)S(1)} %get-tuple-element.25), channel_id=1, source_target_pairs={{16,0},{32,16},{48,32},{64,48},{80,64},{96,80},{112,96},{128,112},... | collective-permute-start | bytes 49160 | tf_op jit(solution)/shard_map/ppermute | solution.py:25
  13.2 3.6 %collective-permute-start = (bf16[1,64,128]{2,1,0:T(8,128)(2,1)S(1)}, bf16[1,64,128]{2,1,0:T(8,128)(2,1)S(1)}, u32[]{:S(2)}, u32[]{:S(2)}) collective-permute-start(bf16[1,64,128]{2,1,0:T(8,128)(2,1)S(1)} %get-tuple-element.26), channel_id=1, source_target_pairs={{0,16},{16,32},{32,48},{48,64},{64,80},{80,96},{96,112},{112,128},... | collective-permute-start | bytes 49160 | tf_op jit(solution)/shard_map/ppermute | solution.py:22
  20.1 28.0 %all-to-all-start = ((bf16[512,8,128]{2,1,0:T(8,128)(2,1)}), bf16[512,8,128]{2,1,0:T(8,128)(2,1)}, u32[]{:S(2)}, u32[]{:S(2)}) async-start(bf16[512,8,128]{2,1,0:T(8,128)(2,1)} %stack.20), calls=%async_computation | async-start | bytes 2097152 | tf_op jit(solution)/shard_map/all_to_all | solution.py:7
  48.1 2.2 reshape_squeeze.3
  52.3 2.4 gather_fusion
  54.7 48.0 %all-to-all-done = bf16[512,8,128]{2,1,0:T(8,128)(2,1)} async-done(((bf16[512,8,128]{2,1,0:T(8,128)(2,1)}), bf16[512,8,128]{2,1,0:T(8,128)(2,1)}, u32[]{:S(2)}, u32[]{:S(2)}) %all-to-all-start) | async-done | bytes 1048608 | tf_op jit(solution)/shard_map/all_to_all | solution.py:7
  102.7 3.9 %fusion.21 = f32[128,1024]{1,0:T(8,128)S(1)} fusion(bf16[512,8,128]{2,1,0:T(8,128)(2,1)} %all-to-all-done, bf16[512,8,8]{2,1,0:T(8,128)(2,1)} %gather_fusion, pred[512]{0:T(512)(128)(4,1)S(1)} %compare_and_fusion.1, bf16[1,1,8,1024]{3,2,1,0:T(8,128)(2,1)S(1)} %copy-done.4), kind=kOutput, calls=%fused_computation.28 | convolution fusion | flops 10519552 | bytes 1655296 | tf_op jit(solution)/shard_map/dot_general | solution.py:62
  108.3 3.9 %collective-permute-start.7 = (f32[1,64,128]{1,2,0:T(8,128)}, f32[1,64,128]{1,2,0:T(8,128)S(1)}, u32[]{:S(2)}, u32[]{:S(2)}) collective-permute-start(f32[1,64,128]{1,2,0:T(8,128)} %get-tuple-element.7), channel_id=1, source_target_pairs={{1,0},{2,1},{3,2},{4,3},{5,4},{6,5},{7,6},{8,7},{9,8},{10,9},{11,1... | collective-permute-start | bytes 98312 | tf_op jit(solution)/shard_map/ppermute | solution.py:25
  114.1 3.1 %collective-permute-start.5 = (f32[1,64,128]{1,2,0:T(8,128)}, f32[1,64,128]{1,2,0:T(8,128)S(1)}, u32[]{:S(2)}, u32[]{:S(2)}) collective-permute-start(f32[1,64,128]{1,2,0:T(8,128)} %get-tuple-element.9), channel_id=1, source_target_pairs={{16,0},{32,16},{48,32},{64,48},{80,64},{96,80},{112,96},{128,112},... | collective-permute-start | bytes 98312 | tf_op jit(solution)/shard_map/ppermute | solution.py:25
  117.2 2.9 %collective-permute-start.4 = (f32[1,64,128]{1,2,0:T(8,128)}, f32[1,64,128]{1,2,0:T(8,128)S(1)}, u32[]{:S(2)}, u32[]{:S(2)}) collective-permute-start(f32[1,64,128]{1,2,0:T(8,128)} %get-tuple-element.10), channel_id=1, source_target_pairs={{0,16},{16,32},{32,48},{48,64},{64,80},{80,96},{96,112},{112,128},... | collective-permute-start | bytes 98312 | tf_op jit(solution)/shard_map/ppermute | solution.py:22
  126.4 4.2 %collective-permute-start.9 = (f32[3,1,16,128]{3,2,1,0:T(8,128)S(1)}, f32[3,1,16,128]{3,2,1,0:T(8,128)S(1)}, u32[]{:S(2)}, u32[]{:S(2)}) collective-permute-start(f32[3,1,16,128]{3,2,1,0:T(8,128)S(1)} %get-tuple-element.17), channel_id=1, source_target_pairs={{0,16},{16,32},{32,48},{48,64},{64,80},{80,96},{96,112},{112,128},... | collective-permute-start | bytes 73736 | tf_op jit(solution)/shard_map/ppermute | solution.py:22
  130.6 1.9 collective-permute-start.8
  132.5 3.2 %collective-permute-done.8 = f32[3,1,16,128]{3,2,1,0:T(8,128)S(1)} collective-permute-done((f32[3,1,16,128]{3,2,1,0:T(8,128)S(1)}, f32[3,1,16,128]{3,2,1,0:T(8,128)S(1)}, u32[]{:S(2)}, u32[]{:S(2)}) %collective-permute-start.8) | collective-permute-done | bytes 24608 | tf_op jit(solution)/shard_map/ppermute | solution.py:25
  135.8 5.8 %collective-permute-start.10 = (f32[3,18,1,128]{3,2,1,0:T(1,128)S(1)}, f32[3,18,1,128]{3,2,1,0:T(1,128)S(1)}, u32[]{:S(2)}, u32[]{:S(2)}) collective-permute-start(f32[3,18,1,128]{3,2,1,0:T(1,128)S(1)} %get-tuple-element.13), channel_id=1, source_target_pairs={{1,0},{2,1},{3,2},{4,3},{5,4},{6,5},{7,6},{8,7},{9,8},{10,9},{11,1... | collective-permute-start | bytes 82952 | tf_op jit(solution)/shard_map/ppermute | solution.py:25
  141.5 1.9 collective-permute-start.11
  143.5 4.8 %collective-permute-done.11 = f32[3,18,1,128]{3,2,1,0:T(1,128)S(1)} collective-permute-done((f32[3,18,1,128]{3,2,1,0:T(1,128)S(1)}, f32[3,18,1,128]{3,2,1,0:T(1,128)S(1)}, u32[]{:S(2)}, u32[]{:S(2)}) %collective-permute-start.11) | collective-permute-done | bytes 27680 | tf_op jit(solution)/shard_map/ppermute | solution.py:22
  149.4 3.4 %collective-permute-start.12 = (bf16[1,64,128]{2,1,0:T(8,128)(2,1)S(1)}, bf16[1,64,128]{2,1,0:T(8,128)(2,1)S(1)}, u32[]{:S(2)}, u32[]{:S(2)}) collective-permute-start(bf16[1,64,128]{2,1,0:T(8,128)(2,1)S(1)} %get-tuple-element.22), channel_id=1, source_target_pairs={{0,16},{16,32},{32,48},{48,64},{64,80},{80,96},{96,112},{112,128},... | collective-permute-start | bytes 49160 | tf_op jit(solution)/shard_map/ppermute | solution.py:22
  152.8 1.9 collective-permute-start.15
  154.7 3.4 %collective-permute-start.14 = (bf16[1,64,128]{2,1,0:T(8,128)(2,1)S(1)}, bf16[1,64,128]{2,1,0:T(8,128)(2,1)S(1)}, u32[]{:S(2)}, u32[]{:S(2)}) collective-permute-start(bf16[1,64,128]{2,1,0:T(8,128)(2,1)S(1)} %get-tuple-element.20), channel_id=1, source_target_pairs={{0,1},{1,2},{2,3},{3,4},{4,5},{5,6},{6,7},{7,8},{8,9},{9,10},{10,1... | collective-permute-start | bytes 49160 | tf_op jit(solution)/shard_map/ppermute | solution.py:22
  158.1 1.9 collective-permute-start.13
  160.1 3.1 %collective-permute-done.13 = bf16[1,64,128]{2,1,0:T(8,128)(2,1)S(1)} collective-permute-done((bf16[1,64,128]{2,1,0:T(8,128)(2,1)S(1)}, bf16[1,64,128]{2,1,0:T(8,128)(2,1)S(1)}, u32[]{:S(2)}, u32[]{:S(2)}) %collective-permute-start.13) | collective-permute-done | bytes 16416 | tf_op jit(solution)/shard_map/ppermute | solution.py:25
  163.7 69.0 %all_to_all.10 = bf16[512,8,128]{2,1,0:T(8,128)(2,1)} all-to-all(bf16[512,8,128]{2,1,0:T(8,128)(2,1)S(1)} %stack.25), channel_id=1, replica_groups=mesh['gx'=32,'gy'=16] {'gx','gy'}, dimensions={0} | all-to-all | bytes 2097152 | tf_op jit(solution)/shard_map/all_to_all | solution.py:7
  232.8 4.7 %fusion.20 = f32[128,1024]{1,0:T(8,128)} fusion(bf16[512,8,128]{2,1,0:T(8,128)(2,1)} %all_to_all.10, bf16[512,8,8]{2,1,0:T(8,128)(2,1)} %gather_fusion, pred[512]{0:T(512)(128)(4,1)S(1)} %copy-done.15, bf16[1,1,8,1024]{3,2,1,0:T(8,128)(2,1)S(1)} %copy-done.5), kind=kOutput, calls=%fused_computation.27 | convolution fusion | flops 10519552 | bytes 1655296 | tf_op jit(solution)/shard_map/dot_general | solution.py:62
  240.1 3.9 %collective-permute-start.19 = (f32[1,64,128]{1,2,0:T(8,128)}, f32[1,64,128]{1,2,0:T(8,128)S(1)}, u32[]{:S(2)}, u32[]{:S(2)}) collective-permute-start(f32[1,64,128]{1,2,0:T(8,128)} %get-tuple-element.3), channel_id=1, source_target_pairs={{1,0},{2,1},{3,2},{4,3},{5,4},{6,5},{7,6},{8,7},{9,8},{10,9},{11,1... | collective-permute-start | bytes 98312 | tf_op jit(solution)/shard_map/ppermute | solution.py:25
  246.0 3.1 %collective-permute-start.17 = (f32[1,64,128]{1,2,0:T(8,128)}, f32[1,64,128]{1,2,0:T(8,128)S(1)}, u32[]{:S(2)}, u32[]{:S(2)}) collective-permute-start(f32[1,64,128]{1,2,0:T(8,128)} %get-tuple-element.5), channel_id=1, source_target_pairs={{16,0},{32,16},{48,32},{64,48},{80,64},{96,80},{112,96},{128,112},... | collective-permute-start | bytes 98312 | tf_op jit(solution)/shard_map/ppermute | solution.py:25
  249.1 2.9 %collective-permute-start.16 = (f32[1,64,128]{1,2,0:T(8,128)}, f32[1,64,128]{1,2,0:T(8,128)S(1)}, u32[]{:S(2)}, u32[]{:S(2)}) collective-permute-start(f32[1,64,128]{1,2,0:T(8,128)} %get-tuple-element.6), channel_id=1, source_target_pairs={{0,16},{16,32},{32,48},{48,64},{64,80},{80,96},{96,112},{112,128},... | collective-permute-start | bytes 98312 | tf_op jit(solution)/shard_map/ppermute | solution.py:22
  260.4 2.4 collective-permute-start.21
  264.7 3.2 %collective-permute-done.20 = f32[3,1,16,128]{3,2,1,0:T(8,128)S(1)} collective-permute-done((f32[3,1,16,128]{3,2,1,0:T(8,128)S(1)}, f32[3,1,16,128]{3,2,1,0:T(8,128)S(1)}, u32[]{:S(2)}, u32[]{:S(2)}) %collective-permute-start.20) | collective-permute-done | bytes 24608 | tf_op jit(solution)/shard_map/ppermute | solution.py:25
  268.0 5.8 %collective-permute-start.22 = (f32[3,18,1,128]{3,2,1,0:T(1,128)S(1)}, f32[3,18,1,128]{3,2,1,0:T(1,128)S(1)}, u32[]{:S(2)}, u32[]{:S(2)}) collective-permute-start(f32[3,18,1,128]{3,2,1,0:T(1,128)S(1)} %get-tuple-element.11), channel_id=1, source_target_pairs={{1,0},{2,1},{3,2},{4,3},{5,4},{6,5},{7,6},{8,7},{9,8},{10,9},{11,1... | collective-permute-start | bytes 82952 | tf_op jit(solution)/shard_map/ppermute | solution.py:25
  275.7 4.8 %collective-permute-done.23 = f32[3,18,1,128]{3,2,1,0:T(1,128)S(1)} collective-permute-done((f32[3,18,1,128]{3,2,1,0:T(1,128)S(1)}, f32[3,18,1,128]{3,2,1,0:T(1,128)S(1)}, u32[]{:S(2)}, u32[]{:S(2)}) %collective-permute-start.23) | collective-permute-done | bytes 27680 | tf_op jit(solution)/shard_map/ppermute | solution.py:22
  (118 shorter events, 37.8 us)
Async XLA Ops:
  0.6 106.0 %copy-start = (bf16[1,1,1024,1024]{3,2,1,0:T(8,128)(2,1)S(1)}, bf16[1,1,1024,1024]{3,2,1,0:T(8,128)(2,1)}, u32[]{:S(2)}) copy-start(bf16[1,1,1024,1024]{3,2,1,0:T(8,128)(2,1)} %param.11) | copy-start | bytes 6291460
  4.1 13.8 %collective-permute-start.3 = (bf16[1,64,128]{2,1,0:T(8,128)(2,1)S(1)}, bf16[1,64,128]{2,1,0:T(8,128)(2,1)S(1)}, u32[]{:S(2)}, u32[]{:S(2)}) collective-permute-start(bf16[1,64,128]{2,1,0:T(8,128)(2,1)S(1)} %get-tuple-element.23), channel_id=1, source_target_pairs={{1,0},{2,1},{3,2},{4,3},{5,4},{6,5},{7,6},{8,7},{9,8},{10,9},{11,1... | collective-permute-start | bytes 49160 | tf_op jit(solution)/shard_map/ppermute | solution.py:25
  8.4 9.5 %collective-permute-start.2 = (bf16[1,64,128]{2,1,0:T(8,128)(2,1)S(1)}, bf16[1,64,128]{2,1,0:T(8,128)(2,1)S(1)}, u32[]{:S(2)}, u32[]{:S(2)}) collective-permute-start(bf16[1,64,128]{2,1,0:T(8,128)(2,1)S(1)} %get-tuple-element.24), channel_id=1, source_target_pairs={{0,1},{1,2},{2,3},{3,4},{4,5},{5,6},{6,7},{7,8},{8,9},{9,10},{10,1... | collective-permute-start | bytes 49160 | tf_op jit(solution)/shard_map/ppermute | solution.py:22
  10.3 7.5 %collective-permute-start.1 = (bf16[1,64,128]{2,1,0:T(8,128)(2,1)S(1)}, bf16[1,64,128]{2,1,0:T(8,128)(2,1)S(1)}, u32[]{:S(2)}, u32[]{:S(2)}) collective-permute-start(bf16[1,64,128]{2,1,0:T(8,128)(2,1)S(1)} %get-tuple-element.25), channel_id=1, source_target_pairs={{16,0},{32,16},{48,32},{64,48},{80,64},{96,80},{112,96},{128,112},... | collective-permute-start | bytes 49160 | tf_op jit(solution)/shard_map/ppermute | solution.py:25
  13.2 34.9 %copy-start.3 = (bf16[1,1,8,4096]{3,2,1,0:T(8,128)(2,1)S(1)}, bf16[1,1,8,4096]{3,2,1,0:T(8,128)(2,1)}, u32[]{:S(2)}) copy-start(bf16[1,1,8,4096]{3,2,1,0:T(8,128)(2,1)} %param.13) | copy-start | bytes 196612
  13.2 4.6 %collective-permute-start = (bf16[1,64,128]{2,1,0:T(8,128)(2,1)S(1)}, bf16[1,64,128]{2,1,0:T(8,128)(2,1)S(1)}, u32[]{:S(2)}, u32[]{:S(2)}) collective-permute-start(bf16[1,64,128]{2,1,0:T(8,128)(2,1)S(1)} %get-tuple-element.26), channel_id=1, source_target_pairs={{0,16},{16,32},{32,48},{48,64},{64,80},{80,96},{96,112},{112,128},... | collective-permute-start | bytes 49160 | tf_op jit(solution)/shard_map/ppermute | solution.py:22
  20.1 82.6 %all-to-all-start = ((bf16[512,8,128]{2,1,0:T(8,128)(2,1)}), bf16[512,8,128]{2,1,0:T(8,128)(2,1)}, u32[]{:S(2)}, u32[]{:S(2)}) async-start(bf16[512,8,128]{2,1,0:T(8,128)(2,1)} %stack.20), calls=%async_computation | async-start | bytes 2097152 | tf_op jit(solution)/shard_map/all_to_all | solution.py:7
  50.3 52.4 %copy-start.4 = (bf16[1,1,8,1024]{3,2,1,0:T(8,128)(2,1)S(1)}, bf16[1,1,8,1024]{3,2,1,0:T(8,128)(2,1)}, u32[]{:S(2)}) copy-start(bf16[1,1,8,1024]{3,2,1,0:T(8,128)(2,1)} %param.12) | copy-start | bytes 49156
  54.7 52.8 %copy-start.14 = (pred[512]{0:T(512)(128)(4,1)}, pred[512]{0:T(512)(128)(4,1)S(1)}, u32[]{:S(2)}) copy-start(pred[512]{0:T(512)(128)(4,1)S(1)} %compare_and_fusion.1) | copy-start | bytes 1540
  108.3 12.6 %collective-permute-start.7 = (f32[1,64,128]{1,2,0:T(8,128)}, f32[1,64,128]{1,2,0:T(8,128)S(1)}, u32[]{:S(2)}, u32[]{:S(2)}) collective-permute-start(f32[1,64,128]{1,2,0:T(8,128)} %get-tuple-element.7), channel_id=1, source_target_pairs={{1,0},{2,1},{3,2},{4,3},{5,4},{6,5},{7,6},{8,7},{9,8},{10,9},{11,1... | collective-permute-start | bytes 98312 | tf_op jit(solution)/shard_map/ppermute | solution.py:25
  112.2 8.8 %collective-permute-start.6 = (f32[1,64,128]{1,2,0:T(8,128)}, f32[1,64,128]{1,2,0:T(8,128)S(1)}, u32[]{:S(2)}, u32[]{:S(2)}) collective-permute-start(f32[1,64,128]{1,2,0:T(8,128)} %get-tuple-element.8), channel_id=1, source_target_pairs={{0,1},{1,2},{2,3},{3,4},{4,5},{5,6},{6,7},{7,8},{8,9},{9,10},{10,1... | collective-permute-start | bytes 98312 | tf_op jit(solution)/shard_map/ppermute | solution.py:22
  114.1 6.9 %collective-permute-start.5 = (f32[1,64,128]{1,2,0:T(8,128)}, f32[1,64,128]{1,2,0:T(8,128)S(1)}, u32[]{:S(2)}, u32[]{:S(2)}) collective-permute-start(f32[1,64,128]{1,2,0:T(8,128)} %get-tuple-element.9), channel_id=1, source_target_pairs={{16,0},{32,16},{48,32},{64,48},{80,64},{96,80},{112,96},{128,112},... | collective-permute-start | bytes 98312 | tf_op jit(solution)/shard_map/ppermute | solution.py:25
  117.2 4.5 %collective-permute-start.4 = (f32[1,64,128]{1,2,0:T(8,128)}, f32[1,64,128]{1,2,0:T(8,128)S(1)}, u32[]{:S(2)}, u32[]{:S(2)}) collective-permute-start(f32[1,64,128]{1,2,0:T(8,128)} %get-tuple-element.10), channel_id=1, source_target_pairs={{0,16},{16,32},{32,48},{48,64},{64,80},{80,96},{96,112},{112,128},... | collective-permute-start | bytes 98312 | tf_op jit(solution)/shard_map/ppermute | solution.py:22
  120.7 27.5 %copy-start.1 = (f32[3,16,16,128]{3,2,1,0:T(8,128)S(1)}, f32[3,16,16,128]{3,2,1,0:T(8,128)}, u32[]{:S(2)}) copy-start(f32[3,16,16,128]{3,2,1,0:T(8,128)} %param.9) | copy-start | bytes 1179652
  124.2 39.0 %copy-start.5 = (bf16[1,1,8,1024]{3,2,1,0:T(8,128)(2,1)S(1)}, bf16[1,1,8,1024]{3,2,1,0:T(8,128)(2,1)}, u32[]{:S(2)}) copy-start(bf16[1,1,8,1024]{3,2,1,0:T(8,128)(2,1)} %param.12) | copy-start | bytes 49156
  126.4 6.1 %collective-permute-start.9 = (f32[3,1,16,128]{3,2,1,0:T(8,128)S(1)}, f32[3,1,16,128]{3,2,1,0:T(8,128)S(1)}, u32[]{:S(2)}, u32[]{:S(2)}) collective-permute-start(f32[3,1,16,128]{3,2,1,0:T(8,128)S(1)} %get-tuple-element.17), channel_id=1, source_target_pairs={{0,16},{16,32},{32,48},{48,64},{64,80},{80,96},{96,112},{112,128},... | collective-permute-start | bytes 73736 | tf_op jit(solution)/shard_map/ppermute | solution.py:22
  130.6 5.1 %collective-permute-start.8 = (f32[3,1,16,128]{3,2,1,0:T(8,128)S(1)}, f32[3,1,16,128]{3,2,1,0:T(8,128)S(1)}, u32[]{:S(2)}, u32[]{:S(2)}) collective-permute-start(f32[3,1,16,128]{3,2,1,0:T(8,128)S(1)} %get-tuple-element.18), channel_id=1, source_target_pairs={{16,0},{32,16},{48,32},{64,48},{80,64},{96,80},{112,96},{128,112},... | collective-permute-start | bytes 73736 | tf_op jit(solution)/shard_map/ppermute | solution.py:25
  135.8 7.7 %collective-permute-start.10 = (f32[3,18,1,128]{3,2,1,0:T(1,128)S(1)}, f32[3,18,1,128]{3,2,1,0:T(1,128)S(1)}, u32[]{:S(2)}, u32[]{:S(2)}) collective-permute-start(f32[3,18,1,128]{3,2,1,0:T(1,128)S(1)} %get-tuple-element.13), channel_id=1, source_target_pairs={{1,0},{2,1},{3,2},{4,3},{5,4},{6,5},{7,6},{8,7},{9,8},{10,9},{11,1... | collective-permute-start | bytes 82952 | tf_op jit(solution)/shard_map/ppermute | solution.py:25
  141.5 6.7 %collective-permute-start.11 = (f32[3,18,1,128]{3,2,1,0:T(1,128)S(1)}, f32[3,18,1,128]{3,2,1,0:T(1,128)S(1)}, u32[]{:S(2)}, u32[]{:S(2)}) collective-permute-start(f32[3,18,1,128]{3,2,1,0:T(1,128)S(1)} %get-tuple-element.14), channel_id=1, source_target_pairs={{0,1},{1,2},{2,3},{3,4},{4,5},{5,6},{6,7},{7,8},{8,9},{9,10},{10,1... | collective-permute-start | bytes 82952 | tf_op jit(solution)/shard_map/ppermute | solution.py:22
  149.4 83.4 %copy-start.15 = (pred[512]{0:T(512)(128)(4,1)S(1)}, pred[512]{0:T(512)(128)(4,1)}, u32[]{:S(2)}) copy-start(pred[512]{0:T(512)(128)(4,1)} %copy-done.14) | copy-start | bytes 1540
  149.4 10.6 %collective-permute-start.12 = (bf16[1,64,128]{2,1,0:T(8,128)(2,1)S(1)}, bf16[1,64,128]{2,1,0:T(8,128)(2,1)S(1)}, u32[]{:S(2)}, u32[]{:S(2)}) collective-permute-start(bf16[1,64,128]{2,1,0:T(8,128)(2,1)S(1)} %get-tuple-element.22), channel_id=1, source_target_pairs={{0,16},{16,32},{32,48},{48,64},{64,80},{80,96},{96,112},{112,128},... | collective-permute-start | bytes 49160 | tf_op jit(solution)/shard_map/ppermute | solution.py:22
  152.8 10.4 %collective-permute-start.15 = (bf16[1,64,128]{2,1,0:T(8,128)(2,1)S(1)}, bf16[1,64,128]{2,1,0:T(8,128)(2,1)S(1)}, u32[]{:S(2)}, u32[]{:S(2)}) collective-permute-start(bf16[1,64,128]{2,1,0:T(8,128)(2,1)S(1)} %get-tuple-element.19), channel_id=1, source_target_pairs={{1,0},{2,1},{3,2},{4,3},{5,4},{6,5},{7,6},{8,7},{9,8},{10,9},{11,1... | collective-permute-start | bytes 49160 | tf_op jit(solution)/shard_map/ppermute | solution.py:25
  154.7 8.4 %collective-permute-start.14 = (bf16[1,64,128]{2,1,0:T(8,128)(2,1)S(1)}, bf16[1,64,128]{2,1,0:T(8,128)(2,1)S(1)}, u32[]{:S(2)}, u32[]{:S(2)}) collective-permute-start(bf16[1,64,128]{2,1,0:T(8,128)(2,1)S(1)} %get-tuple-element.20), channel_id=1, source_target_pairs={{0,1},{1,2},{2,3},{3,4},{4,5},{5,6},{6,7},{7,8},{8,9},{9,10},{10,1... | collective-permute-start | bytes 49160 | tf_op jit(solution)/shard_map/ppermute | solution.py:22
  158.1 5.1 %collective-permute-start.13 = (bf16[1,64,128]{2,1,0:T(8,128)(2,1)S(1)}, bf16[1,64,128]{2,1,0:T(8,128)(2,1)S(1)}, u32[]{:S(2)}, u32[]{:S(2)}) collective-permute-start(bf16[1,64,128]{2,1,0:T(8,128)(2,1)S(1)} %get-tuple-element.21), channel_id=1, source_target_pairs={{16,0},{32,16},{48,32},{64,48},{80,64},{96,80},{112,96},{128,112},... | collective-permute-start | bytes 49160 | tf_op jit(solution)/shard_map/ppermute | solution.py:25
  240.1 13.7 %collective-permute-start.19 = (f32[1,64,128]{1,2,0:T(8,128)}, f32[1,64,128]{1,2,0:T(8,128)S(1)}, u32[]{:S(2)}, u32[]{:S(2)}) collective-permute-start(f32[1,64,128]{1,2,0:T(8,128)} %get-tuple-element.3), channel_id=1, source_target_pairs={{1,0},{2,1},{3,2},{4,3},{5,4},{6,5},{7,6},{8,7},{9,8},{10,9},{11,1... | collective-permute-start | bytes 98312 | tf_op jit(solution)/shard_map/ppermute | solution.py:25
  244.1 11.4 %collective-permute-start.18 = (f32[1,64,128]{1,2,0:T(8,128)}, f32[1,64,128]{1,2,0:T(8,128)S(1)}, u32[]{:S(2)}, u32[]{:S(2)}) collective-permute-start(f32[1,64,128]{1,2,0:T(8,128)} %get-tuple-element.4), channel_id=1, source_target_pairs={{0,1},{1,2},{2,3},{3,4},{4,5},{5,6},{6,7},{7,8},{8,9},{9,10},{10,1... | collective-permute-start | bytes 98312 | tf_op jit(solution)/shard_map/ppermute | solution.py:22
  246.0 9.5 %collective-permute-start.17 = (f32[1,64,128]{1,2,0:T(8,128)}, f32[1,64,128]{1,2,0:T(8,128)S(1)}, u32[]{:S(2)}, u32[]{:S(2)}) collective-permute-start(f32[1,64,128]{1,2,0:T(8,128)} %get-tuple-element.5), channel_id=1, source_target_pairs={{16,0},{32,16},{48,32},{64,48},{80,64},{96,80},{112,96},{128,112},... | collective-permute-start | bytes 98312 | tf_op jit(solution)/shard_map/ppermute | solution.py:25
  249.1 6.5 %collective-permute-start.16 = (f32[1,64,128]{1,2,0:T(8,128)}, f32[1,64,128]{1,2,0:T(8,128)S(1)}, u32[]{:S(2)}, u32[]{:S(2)}) collective-permute-start(f32[1,64,128]{1,2,0:T(8,128)} %get-tuple-element.6), channel_id=1, source_target_pairs={{0,16},{16,32},{32,48},{48,64},{64,80},{80,96},{96,112},{112,128},... | collective-permute-start | bytes 98312 | tf_op jit(solution)/shard_map/ppermute | solution.py:22
  260.4 4.3 %collective-permute-start.21 = (f32[3,1,16,128]{3,2,1,0:T(8,128)S(1)}, f32[3,1,16,128]{3,2,1,0:T(8,128)S(1)}, u32[]{:S(2)}, u32[]{:S(2)}) collective-permute-start(f32[3,1,16,128]{3,2,1,0:T(8,128)S(1)} %get-tuple-element.15), channel_id=1, source_target_pairs={{0,16},{16,32},{32,48},{48,64},{64,80},{80,96},{96,112},{112,128},... | collective-permute-start | bytes 73736 | tf_op jit(solution)/shard_map/ppermute | solution.py:22
  262.8 5.1 %collective-permute-start.20 = (f32[3,1,16,128]{3,2,1,0:T(8,128)S(1)}, f32[3,1,16,128]{3,2,1,0:T(8,128)S(1)}, u32[]{:S(2)}, u32[]{:S(2)}) collective-permute-start(f32[3,1,16,128]{3,2,1,0:T(8,128)S(1)} %get-tuple-element.16), channel_id=1, source_target_pairs={{16,0},{32,16},{48,32},{64,48},{80,64},{96,80},{112,96},{128,112},... | collective-permute-start | bytes 73736 | tf_op jit(solution)/shard_map/ppermute | solution.py:25
  268.0 7.7 %collective-permute-start.22 = (f32[3,18,1,128]{3,2,1,0:T(1,128)S(1)}, f32[3,18,1,128]{3,2,1,0:T(1,128)S(1)}, u32[]{:S(2)}, u32[]{:S(2)}) collective-permute-start(f32[3,18,1,128]{3,2,1,0:T(1,128)S(1)} %get-tuple-element.11), channel_id=1, source_target_pairs={{1,0},{2,1},{3,2},{4,3},{5,4},{6,5},{7,6},{8,7},{9,8},{10,9},{11,1... | collective-permute-start | bytes 82952 | tf_op jit(solution)/shard_map/ppermute | solution.py:25
  273.7 6.7 %collective-permute-start.23 = (f32[3,18,1,128]{3,2,1,0:T(1,128)S(1)}, f32[3,18,1,128]{3,2,1,0:T(1,128)S(1)}, u32[]{:S(2)}, u32[]{:S(2)}) collective-permute-start(f32[3,18,1,128]{3,2,1,0:T(1,128)S(1)} %get-tuple-element.12), channel_id=1, source_target_pairs={{0,1},{1,2},{2,3},{3,4},{4,5},{5,6},{6,7},{7,8},{8,9},{9,10},{10,1... | collective-permute-start | bytes 82952 | tf_op jit(solution)/shard_map/ppermute | solution.py:22
  (9 other events, 111.8 us)
